TPU v7x, 512 devices: a whole 4x8x8 slice. The times are simulated.
512 devices in a mesh: lat: 128 (over z, y, core), rad: 4 (over x).
Axes of the slice: x: 4, y: 8, z: 8, core: 2. Of those that a mesh axis runs over, the one named last changes fastest.
Arguments:
- displacement: float32 [64, 98304], P('rad', 'lat'), may hold values from -6 to 6
- surface_load: float32 [64, 98304], P('rad', 'lat'), may hold values from -6 to 6
- dens_grad: float32 [64, 98304], P('rad', 'lat'), may hold values from 0.5 to 2
- dens_ref: float32 [64], P('rad'), may hold values from 0.5 to 2
- relax_rate: float32 [64, 98304], P('rad', 'lat'), may hold values from 0.02 to 0.2
- basis: bfloat16 [2432, 98304], P(None, 'lat'), may hold values from -0.078125 to 0.078125
- neighbours: int32 [4, 98304], P(None, 'lat'), may hold values from 0 to 767
- green: float32 [49, 64, 64], replicated, may hold values from -6 to 6
Outputs:
- relaxed: float32 [64, 98304], P('rad', 'lat')
- step_sizes: float32 [3], replicated
Inputs may be any that keep to these rules, and one draw needn't show every extreme that they name: `neighbours`: indices of columns inside the same tile of 768 columns.
All inputs are finite; a program needn't handle non-finite values.
Results may differ from a plain program's by a relative error of at most 0.0045.
Values may be sent and summed in bfloat16 or wider, within the bound.
A program may use at most 64 MiB of HBM per device.

v0:
```python
import functools

import jax
import jax.numpy as jnp
from jax import lax
from jax.experimental import pallas as pl
from jax.experimental.pallas import tpu as pltpu
from jax.sharding import Mesh
from jax.sharding import PartitionSpec as P

DEG = 48
L = 64
ITERS = 3
KH = 2401
NZ, NY, NC, NX = 8, 8, 2, 4
GROUPS = 19
LANES = 128
AXES = ("lz", "ly", "lc", "rad")
LAT = AXES[:3]
MESH = pl.DeviceIdType.MESH
NT = (((1,), (1,)), ((), ()))
NN = (((1,), (0,)), ((), ()))
F32 = jnp.float32
BF16 = jnp.bfloat16

PLANE = sorted(
    [(dz, dy) for dz in range(NZ) for dy in range(NY) if dz or dy],
    key=lambda o: -(min(o[0], NZ - o[0]) + min(o[1], NY - o[1])),
)


def group_chip(g):
    if g < 8:
        return g, g % 4
    if g < 16:
        return g - 8, (g - 8 + 2) % 4
    return (g - 16) * 3, ((g - 16) * 3 + 1) % 4


def owned_group(z, y, core):
    b = y // 2
    g = jnp.where(b == z % 4, z, -1)
    g = jnp.where(b == (z + 2) % 4, z + 8, g)
    extra = (b == (z + 1) % 4) & (z % 3 == 0)
    g = jnp.where(extra, z // 3 + 16, g)
    return jnp.where(y % 2 == core, g, -1)


def kernel(
    disp, load, grad, dref, rate, basis_hbm, nbr, green_hbm,
    out, sizes,
    basis, green, u_s, ld_s, rt_s, gr_s, nbr_s, dref_s, hsend, hrecv, count, gexp, onehot,
    base, part, rsbuf, xsend, xbuf, lsend, lbuf, fsend, fplane, fsend2, fx, sq_s,
    in_sem, hs_sem, hr_sem, rs_ssem, rs_rsem, x_ssem, x_rsem, ag_ssem, ag_rsem,
    f_ssem, f_rsem, f2_ssem, f2_rsem,
):
    z, y, c, x = (lax.axis_index(a) for a in AXES)
    chip = z * NY + y
    g_own = owned_group(z, y, c)
    owner = g_own >= 0
    other_y = 2 * (y // 2) + (1 - y % 2)

    plane_ids = [((z + dz) % NZ, (y + dy) % NY, c, x) for dz, dy in PLANE]
    same = [(z, y, c, (x + d) % NX) for d in (2, 1, 3)]
    cross = [(z, other_y, 1 - c, (x + d) % NX) for d in (2, 1, 3, 0)]
    near_ids = same + cross

    barrier = pltpu.get_barrier_semaphore()
    for dev in plane_ids + near_ids:
        pl.semaphore_signal(barrier, inc=1, device_id=dev, device_id_type=MESH)

    loads = [
        pltpu.make_async_copy(nbr, nbr_s, in_sem.at[0]),
        pltpu.make_async_copy(disp, u_s.at[pl.ds(0, 16)], in_sem.at[1]),
        pltpu.make_async_copy(load, ld_s.at[pl.ds(0, 16)], in_sem.at[2]),
        pltpu.make_async_copy(rate, rt_s.at[pl.ds(0, 16)], in_sem.at[3]),
        pltpu.make_async_copy(grad, gr_s, in_sem.at[4]),
        pltpu.make_async_copy(dref, dref_s, in_sem.at[5]),
        pltpu.make_async_copy(green_hbm, green, in_sem.at[6]),
        pltpu.make_async_copy(basis_hbm, basis, in_sem.at[7]),
    ]
    for copy in loads:
        copy.start()

    loads[0].wait()

    def count_rows(block, carry):
        start = pl.multiple_of(block * 64, 64)
        rows = lax.broadcasted_iota(jnp.int32, (64, 768), 0) + start
        total = jnp.zeros((64, 768), F32)
        for j in range(4):
            total = total + jnp.where(nbr_s[j : j + 1, :] == rows, 1.0, 0.0)
        count[pl.ds(start, 64), :] = total.astype(BF16)
        return carry

    lax.fori_loop(0, 12, count_rows, 0)

    for copy in loads[1:7]:
        copy.wait()

    @pl.when(owner)
    def _():
        k = g_own * LANES + lax.broadcasted_iota(jnp.int32, (LANES, LANES), 1)
        d = lax.broadcasted_iota(jnp.int32, (LANES, LANES), 0) % 64
        hit = (k >= d * d) & (k < (d + 1) * (d + 1)) & (k < KH)
        onehot[...] = jnp.where(hit, 1.0, 0.0).astype(BF16)

        def green_row(i):
            layer = x * 16 + i
            inside = (layer >= 0) & (layer < L)
            at = jnp.where(inside, layer, 0)
            rows = green[pl.ds(at, DEG + 1, stride=L), :]
            rows = jnp.where(inside, rows, 0.0)
            return jnp.concatenate([rows, jnp.zeros((64 - DEG - 1, L), F32)], axis=0)

        def expand(slot, i):
            layer = x * 16 + i
            inside = (layer >= 0) & (layer < L)
            diff = (green_row(i + 1) - green_row(i - 1)) * 0.5
            diff = jnp.where(inside, diff, 0.0).T
            high = diff.astype(BF16).astype(F32)
            both = jnp.concatenate([high, diff - high], axis=1).astype(BF16)
            gexp[slot] = lax.dot_general(both, onehot[...], NN, preferred_element_type=F32)

        def expand_main(i, carry):
            expand(i, i)
            return carry

        lax.fori_loop(0, 16, expand_main, 0)
        expand(16, -1)
        expand(17, 16)

    zeros5 = jnp.zeros((5, 768), F32)
    hsend[0] = jnp.concatenate([u_s[15:16], ld_s[15:16], rt_s[15:16], zeros5], axis=0)
    hsend[1] = jnp.concatenate([u_s[0:1], ld_s[0:1], rt_s[0:1], zeros5], axis=0)

    pl.semaphore_wait(barrier, len(plane_ids) + len(near_ids))

    halos = []
    for side, step in ((0, 1), (1, NX - 1)):
        halos.append(
            pltpu.make_async_remote_copy(
                src_ref=hsend.at[side], dst_ref=hrecv.at[side],
                send_sem=hs_sem.at[side], recv_sem=hr_sem.at[side],
                device_id=(z, y, c, (x + step) % NX), device_id_type=MESH,
            )
        )
    for copy in halos:
        copy.start()
    loads[7].wait()
    eye = lax.broadcasted_iota(jnp.int32, (16, 16), 0) == lax.broadcasted_iota(jnp.int32, (16, 16), 1)
    half_ref = 0.5 * jnp.sum(jnp.where(eye, dref_s[...], 0.0), axis=1, keepdims=True)
    for copy in halos:
        copy.wait()
    before = jnp.where(x > 0, hrecv[0], 0.0)
    after = jnp.where(x < NX - 1, hrecv[1], 0.0)
    zeros6 = jnp.zeros((6, 768), F32)
    for row, ref in enumerate((u_s, ld_s, rt_s)):
        ref[16:24] = jnp.concatenate([before[row : row + 1], after[row : row + 1], zeros6], axis=0)

    def step(it, carry):
        u = u_s[...]
        inner = u[0:16]
        upper = jnp.concatenate([u[1:16], u[17:18]], axis=0)
        lower = jnp.concatenate([u[16:17], u[0:15]], axis=0)
        rho = (gr_s[...] * inner + half_ref * (upper - lower)).astype(BF16)

        for g in range(GROUPS):
            tile = lax.dot_general(
                rho, basis[g * LANES : (g + 1) * LANES, :], NT, preferred_element_type=F32
            )
            part[it, g] = tile.astype(BF16)
            gz, gb = group_chip(g)
            gy = gb * 2 + c

            @pl.when(g_own != g)
            def _():
                pltpu.make_async_remote_copy(
                    src_ref=part.at[it, g], dst_ref=rsbuf.at[it, chip],
                    send_sem=rs_ssem.at[it], recv_sem=rs_rsem.at[it],
                    device_id=(gz, gy, c, x), device_id_type=MESH,
                ).start()

            @pl.when(g_own == g)
            def _():
                rsbuf[it, chip] = tile.astype(BF16)

        high = u.astype(BF16).astype(F32)
        halves = jnp.concatenate([high, u - high], axis=0).astype(BF16)
        gathered = lax.dot_general(halves, count[...], NN, preferred_element_type=F32)
        lap = gathered[0:24] + gathered[24:48] - 4.0 * u
        base[...] = ld_s[...] + lap - u

        @pl.when(owner)
        def _():
            incoming = rsbuf.at[it, pl.ds(0, NZ * NY - 1)]
            pltpu.make_async_copy(incoming, incoming, rs_rsem.at[it]).wait()
            sums = [jnp.zeros((16, LANES), F32) for _ in range(4)]
            for s in range(NZ * NY):
                sums[s % 4] = sums[s % 4] + rsbuf[it, s].astype(F32)
            total = (sums[0] + sums[1]) + (sums[2] + sums[3])
            xsend[it] = total
            me = x * NC + c
            for dev in near_ids:
                pltpu.make_async_remote_copy(
                    src_ref=xsend.at[it], dst_ref=xbuf.at[it, me],
                    send_sem=x_ssem.at[it], recv_sem=x_rsem.at[it],
                    device_id=dev, device_id_type=MESH,
                ).start()
            xbuf[it, me] = total
            others = xbuf.at[it, pl.ds(0, NX * NC - 1)]
            pltpu.make_async_copy(others, others, x_rsem.at[it]).wait()
            coefs = jnp.concatenate(
                [xbuf[it, 2 * b] + xbuf[it, 2 * b + 1] for b in range(NX)], axis=0
            )
            rows = [jnp.sum(gexp[i] * coefs, axis=0, keepdims=True) for i in range(18)]
            rows.append(jnp.zeros((14, LANES), F32))
            phi = jnp.concatenate(rows, axis=0).astype(BF16)
            lsend[it] = phi
            for dev in plane_ids:
                pltpu.make_async_remote_copy(
                    src_ref=lsend.at[it], dst_ref=lbuf.at[it, g_own],
                    send_sem=ag_ssem.at[it], recv_sem=ag_rsem.at[it, g_own],
                    device_id=dev, device_id_type=MESH,
                ).start()
            lbuf[it, g_own] = phi

        force = jnp.zeros((32, 768), F32)
        for g in range(GROUPS):
            @pl.when(g_own != g)
            def _():
                pltpu.make_async_copy(lbuf.at[it, g], lbuf.at[it, g], ag_rsem.at[it, g]).wait()

            force = force + lax.dot_general(
                lbuf[it, g], basis[g * LANES : (g + 1) * LANES, :], NN, preferred_element_type=F32
            )
        delta = rt_s[...] * (base[...] + force[0:24])
        u_s[...] = u_s[...] + delta
        square = delta[0:16] * delta[0:16]
        square = jnp.sum(jnp.sum(square, axis=0, keepdims=True), axis=1, keepdims=True)
        lane = lax.broadcasted_iota(jnp.int32, (1, LANES), 1)
        sq_s[...] = jnp.where(lane == it, square, sq_s[...])
        return carry

    sq_s[...] = jnp.zeros((1, LANES), F32)
    lax.fori_loop(0, ITERS, step, 0)

    fsend[0] = sq_s[...]
    for dev in plane_ids:
        pltpu.make_async_remote_copy(
            src_ref=fsend.at[0], dst_ref=fplane.at[chip], send_sem=f_ssem, recv_sem=f_rsem,
            device_id=dev, device_id_type=MESH,
        ).start()
    fplane[chip] = sq_s[...]
    out[...] = u_s[0:16]
    others = fplane.at[pl.ds(0, NZ * NY - 1)]
    pltpu.make_async_copy(others, others, f_rsem).wait()
    total = jnp.zeros((1, LANES), F32)
    for s in range(NZ * NY):
        total = total + fplane[s]
    fsend2[0] = total
    me = x * NC + c
    for dev in near_ids:
        pltpu.make_async_remote_copy(
            src_ref=fsend2.at[0], dst_ref=fx.at[me], send_sem=f2_ssem, recv_sem=f2_rsem,
            device_id=dev, device_id_type=MESH,
        ).start()
    fx[me] = total
    others2 = fx.at[pl.ds(0, NX * NC - 1)]
    pltpu.make_async_copy(others2, others2, f2_rsem).wait()
    total = jnp.zeros((1, LANES), F32)
    for s in range(NX * NC):
        total = total + fx[s]
    sizes[...] = jnp.sqrt(total * (1.0 / (L * 768 * NZ * NY * NC)))

    pltpu.make_async_copy(others, others, f_ssem).wait()
    pltpu.make_async_copy(others2, others2, f2_ssem).wait()
    for it in range(ITERS):
        @pl.when(owner)
        def _():
            sent = part.at[it, pl.ds(0, GROUPS - 1)]
            pltpu.make_async_copy(sent, sent, rs_ssem.at[it]).wait()
            sent = xbuf.at[it, pl.ds(0, NX * NC - 1)]
            pltpu.make_async_copy(sent, sent, x_ssem.at[it]).wait()
            sent = rsbuf.at[pl.ds(0, 2), pl.ds(0, NZ * NY - 1)]
            pltpu.make_async_copy(sent, sent, ag_ssem.at[it]).wait()

        @pl.when(jnp.logical_not(owner))
        def _():
            sent = part.at[it]
            pltpu.make_async_copy(sent, sent, rs_ssem.at[it]).wait()


def local(displacement, surface_load, dens_grad, dens_ref, relax_rate, basis, neighbours, green):
    vmem = pltpu.VMEM
    dma = pltpu.SemaphoreType.DMA
    scratch = [
        vmem((2432, 768), BF16),
        vmem(((DEG + 1) * L, L), F32),
        vmem((24, 768), F32),
        vmem((24, 768), F32),
        vmem((24, 768), F32),
        vmem((16, 768), F32),
        vmem((4, 768), jnp.int32),
        vmem((1, 16), F32),
        vmem((2, 8, 768), F32),
        vmem((2, 8, 768), F32),
        vmem((768, 768), BF16),
        vmem((18, 64, LANES), F32),
        vmem((LANES, LANES), BF16),
        vmem((24, 768), F32),
        vmem((ITERS, GROUPS, 16, LANES), BF16),
        vmem((ITERS, NZ * NY, 16, LANES), BF16),
        vmem((ITERS, 16, LANES), F32),
        vmem((ITERS, NX * NC, 16, LANES), F32),
        vmem((ITERS, 32, LANES), BF16),
        vmem((ITERS, GROUPS, 32, LANES), BF16),
        vmem((1, 1, LANES), F32),
        vmem((NZ * NY, 1, LANES), F32),
        vmem((1, 1, LANES), F32),
        vmem((NX * NC, 1, LANES), F32),
        vmem((1, LANES), F32),
        dma((8,)), dma((2,)), dma((2,)),
        dma((ITERS,)), dma((ITERS,)), dma((ITERS,)), dma((ITERS,)), dma((ITERS,)),
        dma((ITERS, GROUPS)),
        dma, dma, dma, dma,
    ]
    relaxed, sizes = pl.pallas_call(
        kernel,
        out_shape=(
            jax.ShapeDtypeStruct((16, 768), F32),
            jax.ShapeDtypeStruct((1, LANES), F32),
        ),
        in_specs=[pl.BlockSpec(memory_space=pl.ANY)] * 8,
        out_specs=(
            pl.BlockSpec(memory_space=pltpu.VMEM),
            pl.BlockSpec(memory_space=pltpu.VMEM),
        ),
        scratch_shapes=scratch,
        compiler_params=pltpu.CompilerParams(
            collective_id=0, has_side_effects=True, vmem_limit_bytes=56 << 20
        ),
        name="relaxation",
    )(
        displacement,
        surface_load,
        dens_grad,
        dens_ref.reshape(1, 16),
        relax_rate,
        basis,
        neighbours,
        green.reshape((DEG + 1) * L, L),
    )
    return relaxed, sizes[0, :ITERS]


def solution(mesh):
    torus = Mesh(mesh.devices.reshape(NZ, NY, NC, NX), AXES)
    return jax.shard_map(
        local,
        mesh=torus,
        in_specs=(
            P("rad", LAT),
            P("rad", LAT),
            P("rad", LAT),
            P("rad"),
            P("rad", LAT),
            P(None, LAT),
            P(None, LAT),
            P(),
        ),
        out_specs=(P("rad", LAT), P()),
        check_vma=False,
    )
```

profile of v0, /device:TPU:1, one launch (start us, length us, event | category | flops | bytes accessed | tf_op | source)
XLA Modules:
  0.0 107.9 jit_solution(6468982241482742156)
XLA Ops:
  0.6 104.7 %relaxation.1 = (f32[16,768]{1,0:T(8,128)}, f32[1,128]{1,0:T(1,128)}) custom-call(f32[16,768]{1,0:T(8,128)} %disp.1, f32[16,768]{1,0:T(8,128)} %load.1, f32[16,768]{1,0:T(8,128)} %grad.1, f32[1,16]{1,0:T(1,128)} %bitcast.5, f32[16,768]{1,0:T(8,128)} %rate.1, bf16[2432,768]{1,0:T(8,128)(2,1)} %basis_hbm.1, s32[4,768]{1,0:T(4,128)} %nbr.1, f32[3136,64]{1,0:T(8,128)} %bitcast.4), custom_call_target="tpu_custom_call" | custom-call | tf_op jit(solution)/shard_map/relaxation/pallas_call | solution.py:328
  105.4 1.1 %slice_bitcast_fusion = f32[3]{0:T(128)} fusion(f32[1,128]{1,0:T(1,128)} %get-tuple-element.5), kind=kLoop, calls=%fused_computation | loop fusion | bytes 24 | tf_op jit(solution)/shard_map/squeeze | solution.py:354
  106.5 1.4 %copy.11 = f32[16,768]{1,0:T(8,128)} copy(f32[16,768]{1,0:T(8,128)} %get-tuple-element.8) | data formatting | bytes 98304
where the time goes:
time: 108 us
  Pallas kernels  105 us (97%)
  local copies, waits for them, and re-layouts  2.57 us (2%)
    pallas_call x1, Pallas kernels, local(): pl.pallas_call(kernel, out_shape=(jax.ShapeDtypeStruct((16, 768), F32), j...  105 us

commit v1 on v0

v1 whole, which is shorter than its diff:
```python
import jax
import jax.numpy as jnp
from jax import lax
from jax.experimental import pallas as pl
from jax.experimental.pallas import tpu as pltpu
from jax.sharding import Mesh
from jax.sharding import PartitionSpec as P

DEG = 48
L = 64
ITERS = 3
KH = 2401
NZ, NY, NC, NX = 8, 8, 2, 4
GROUPS = 19
LANES = 128
AXES = ("lz", "ly", "lc", "rad")
LAT = AXES[:3]
MESH = pl.DeviceIdType.MESH
NT = (((1,), (1,)), ((), ()))
NN = (((1,), (0,)), ((), ()))
F32 = jnp.float32
BF16 = jnp.bfloat16

PLANE = sorted(
    [(dz, dy) for dz in range(NZ) for dy in range(NY) if dz or dy],
    key=lambda o: -(min(o[0], NZ - o[0]) + min(o[1], NY - o[1])),
)


def group_chip(g):
    if g < 8:
        return g, g % 4
    if g < 16:
        return g - 8, (g - 8 + 2) % 4
    return (g - 16) * 3, ((g - 16) * 3 + 1) % 4


def owned_group(z, y, core):
    b = y // 2
    g = jnp.where(b == z % 4, z, -1)
    g = jnp.where(b == (z + 2) % 4, z + 8, g)
    extra = (b == (z + 1) % 4) & (z % 3 == 0)
    g = jnp.where(extra, z // 3 + 16, g)
    return jnp.where(y % 2 == core, g, -1)


def kernel(
    disp, load, grad, dref, rate, basis_hbm, nbr, green_hbm,
    out, sizes,
    basis, green, u_s, ld_s, rt_s, gr_s, nbr_s, dref_s, count, gexp, onehot,
    base, part, edge, rsbuf, edgebuf, xsend, xbuf, lsend, lbuf, fsend, fplane, fsend2, fx, sq_s,
    in_sem, out_sem, rs_ssem, rs_rsem, e_ssem, e_rsem, x_ssem, x_rsem, ag_ssem, ag_rsem,
    f_ssem, f_rsem, f2_ssem, f2_rsem,
):
    z, y, c, x = (lax.axis_index(a) for a in AXES)
    chip = z * NY + y
    g_own = owned_group(z, y, c)
    owner = g_own >= 0
    other_y = 2 * (y // 2) + (1 - y % 2)

    plane_ids = [((z + dz) % NZ, (y + dy) % NY, c, x) for dz, dy in PLANE]
    same = [(z, y, c, (x + d) % NX) for d in (2, 1, 3)]
    cross = [(z, other_y, 1 - c, (x + d) % NX) for d in (2, 1, 3, 0)]
    near_ids = same + cross

    barrier = pltpu.get_barrier_semaphore()
    for dev in plane_ids + near_ids:
        pl.semaphore_signal(barrier, inc=1, device_id=dev, device_id_type=MESH)

    loads = [
        pltpu.make_async_copy(disp, u_s, in_sem.at[0]),
        pltpu.make_async_copy(grad, gr_s, in_sem.at[1]),
        pltpu.make_async_copy(dref, dref_s, in_sem.at[2]),
        pltpu.make_async_copy(basis_hbm, basis, in_sem.at[3]),
        pltpu.make_async_copy(nbr, nbr_s, in_sem.at[4]),
        pltpu.make_async_copy(green_hbm, green, in_sem.at[5]),
        pltpu.make_async_copy(load, ld_s, in_sem.at[6]),
        pltpu.make_async_copy(rate, rt_s, in_sem.at[7]),
    ]
    for copy in loads:
        copy.start()

    def count_rows(block, carry):
        start = pl.multiple_of(block * 64, 64)
        rows = lax.broadcasted_iota(jnp.int32, (64, 768), 0) + start
        total = jnp.zeros((64, 768), F32)
        for j in range(4):
            total = total + jnp.where(nbr_s[j : j + 1, :] == rows, 1.0, 0.0)
        count[pl.ds(start, 64), :] = total.astype(BF16)
        return carry

    def green_row(i):
        layer = x * 16 + i
        inside = (layer >= 0) & (layer < L)
        at = jnp.where(inside, layer, 0)
        rows = green[pl.ds(at, DEG + 1, stride=L), :]
        rows = jnp.where(inside, rows, 0.0)
        return jnp.concatenate([rows, jnp.zeros((64 - DEG - 1, L), F32)], axis=0)

    def expand(i, carry):
        diff = ((green_row(i + 1) - green_row(i - 1)) * 0.5).T
        high = diff.astype(BF16).astype(F32)
        both = jnp.concatenate([high, diff - high], axis=1).astype(BF16)
        gexp[i] = lax.dot_general(both, onehot[...], NN, preferred_element_type=F32)
        return carry

    for copy in loads[:4]:
        copy.wait()
    eye = lax.broadcasted_iota(jnp.int32, (16, 16), 0) == lax.broadcasted_iota(jnp.int32, (16, 16), 1)
    half_ref = 0.5 * jnp.sum(jnp.where(eye, dref_s[...], 0.0), axis=1, keepdims=True)
    ends = jnp.concatenate(
        [
            jnp.broadcast_to(half_ref[0:1], (1, LANES)),
            jnp.broadcast_to(half_ref[15:16], (1, LANES)),
            jnp.zeros((4, LANES), F32),
        ],
        axis=0,
    )
    sq_s[...] = jnp.zeros((1, LANES), F32)

    pl.semaphore_wait(barrier, len(plane_ids) + len(near_ids))

    def step(it, carry):
        u = u_s[...]
        line = jnp.zeros((1, 768), F32)
        upper = jnp.concatenate([u[1:16], line], axis=0)
        lower = jnp.concatenate([line, u[0:15]], axis=0)
        rho = gr_s[...] * u + half_ref * (upper - lower)
        lines = jnp.concatenate([rho, u[0:1], u[15:16], jnp.zeros((14, 768), F32)], axis=0)
        lines = lines.astype(BF16)

        for g in range(GROUPS):
            tile = lax.dot_general(
                lines, basis[g * LANES : (g + 1) * LANES, :], NT, preferred_element_type=F32
            )
            part[it, g] = tile[0:16].astype(BF16)
            edge[it, g] = tile[16:18]
            gz, gb = group_chip(g)
            dev = (gz, gb * 2 + c, c, x)

            @pl.when(g_own != g)
            def _():
                pltpu.make_async_remote_copy(
                    src_ref=part.at[it, g], dst_ref=rsbuf.at[it, chip],
                    send_sem=rs_ssem.at[it], recv_sem=rs_rsem.at[it],
                    device_id=dev, device_id_type=MESH,
                ).start()
                pltpu.make_async_remote_copy(
                    src_ref=edge.at[it, g], dst_ref=edgebuf.at[it, chip],
                    send_sem=e_ssem.at[it], recv_sem=e_rsem.at[it],
                    device_id=dev, device_id_type=MESH,
                ).start()

            @pl.when(g_own == g)
            def _():
                rsbuf[it, chip] = tile[0:16].astype(BF16)
                edgebuf[it, chip] = tile[16:18]

        @pl.when(it == 0)
        def _():
            for copy in loads[4:]:
                copy.wait()
            lax.fori_loop(0, 12, count_rows, 0)

            @pl.when(owner)
            def _():
                k = g_own * LANES + lax.broadcasted_iota(jnp.int32, (LANES, LANES), 1)
                d = lax.broadcasted_iota(jnp.int32, (LANES, LANES), 0) % 64
                hit = (k >= d * d) & (k < (d + 1) * (d + 1)) & (k < KH)
                onehot[...] = jnp.where(hit, 1.0, 0.0).astype(BF16)
                lax.fori_loop(0, 16, expand, 0)

        high = u.astype(BF16).astype(F32)
        halves = jnp.concatenate([high, u - high], axis=0).astype(BF16)
        gathered = lax.dot_general(halves, count[...], NN, preferred_element_type=F32)
        lap = gathered[0:16] + gathered[16:32] - 4.0 * u
        base[...] = ld_s[...] + lap - u

        @pl.when(owner)
        def _():
            incoming = rsbuf.at[it, pl.ds(0, NZ * NY - 1)]
            pltpu.make_async_copy(incoming, incoming, rs_rsem.at[it]).wait()
            sums = [jnp.zeros((16, LANES), F32) for _ in range(4)]
            for s in range(NZ * NY):
                sums[s % 4] = sums[s % 4] + rsbuf[it, s].astype(F32)
            total = (sums[0] + sums[1]) + (sums[2] + sums[3])
            edges = edgebuf.at[it, pl.ds(0, NZ * NY - 1)]
            pltpu.make_async_copy(edges, edges, e_rsem.at[it]).wait()
            sums = [jnp.zeros((2, LANES), F32) for _ in range(4)]
            for s in range(NZ * NY):
                sums[s % 4] = sums[s % 4] + edgebuf[it, s]
            edge_total = (sums[0] + sums[1]) + (sums[2] + sums[3])
            total = jnp.concatenate([total, edge_total, ends], axis=0)
            xsend[it] = total
            me = x * NC + c
            for dev in near_ids:
                pltpu.make_async_remote_copy(
                    src_ref=xsend.at[it], dst_ref=xbuf.at[it, me],
                    send_sem=x_ssem.at[it], recv_sem=x_rsem.at[it],
                    device_id=dev, device_id_type=MESH,
                ).start()
            xbuf[it, me] = total
            others = xbuf.at[it, pl.ds(0, NX * NC - 1)]
            pltpu.make_async_copy(others, others, x_rsem.at[it]).wait()
            blocks = [xbuf[it, 2 * b] + xbuf[it, 2 * b + 1] for b in range(NX)]
            rows = []
            for b in range(NX):
                first, last = jnp.zeros((1, LANES), F32), jnp.zeros((1, LANES), F32)
                if b > 0:
                    first = -0.5 * blocks[b][18:19] * blocks[b - 1][17:18]
                if b < NX - 1:
                    last = 0.5 * blocks[b][19:20] * blocks[b + 1][16:17]
                mid = jnp.zeros((14, LANES), F32)
                rows.append(blocks[b][0:16] + jnp.concatenate([first, mid, last], axis=0))
            coefs = jnp.concatenate(rows, axis=0)
            rows = [jnp.sum(gexp[i] * coefs, axis=0, keepdims=True) for i in range(16)]
            phi = jnp.concatenate(rows, axis=0).astype(BF16)
            lsend[it] = phi
            for dev in plane_ids:
                pltpu.make_async_remote_copy(
                    src_ref=lsend.at[it], dst_ref=lbuf.at[it, g_own],
                    send_sem=ag_ssem.at[it], recv_sem=ag_rsem.at[it, g_own],
                    device_id=dev, device_id_type=MESH,
                ).start()
            lbuf[it, g_own] = phi

        force = jnp.zeros((16, 768), F32)
        for g in range(GROUPS):
            @pl.when(g_own != g)
            def _():
                pltpu.make_async_copy(lbuf.at[it, g], lbuf.at[it, g], ag_rsem.at[it, g]).wait()

            force = force + lax.dot_general(
                lbuf[it, g], basis[g * LANES : (g + 1) * LANES, :], NN, preferred_element_type=F32
            )
        delta = rt_s[...] * (base[...] + force)
        u_s[...] = u_s[...] + delta
        square = delta * delta
        square = jnp.sum(jnp.sum(square, axis=0, keepdims=True), axis=1, keepdims=True)
        lane = lax.broadcasted_iota(jnp.int32, (1, LANES), 1)
        sq_s[...] = jnp.where(lane == it, square, sq_s[...])
        return carry

    lax.fori_loop(0, ITERS, step, 0)
    result = pltpu.make_async_copy(u_s, out, out_sem)
    result.start()

    fsend[0] = sq_s[...]
    for dev in plane_ids:
        pltpu.make_async_remote_copy(
            src_ref=fsend.at[0], dst_ref=fplane.at[chip], send_sem=f_ssem, recv_sem=f_rsem,
            device_id=dev, device_id_type=MESH,
        ).start()
    fplane[chip] = sq_s[...]
    others = fplane.at[pl.ds(0, NZ * NY - 1)]
    pltpu.make_async_copy(others, others, f_rsem).wait()
    total = jnp.zeros((1, LANES), F32)
    for s in range(NZ * NY):
        total = total + fplane[s]
    fsend2[0] = total
    me = x * NC + c
    for dev in near_ids:
        pltpu.make_async_remote_copy(
            src_ref=fsend2.at[0], dst_ref=fx.at[me], send_sem=f2_ssem, recv_sem=f2_rsem,
            device_id=dev, device_id_type=MESH,
        ).start()
    fx[me] = total
    others2 = fx.at[pl.ds(0, NX * NC - 1)]
    pltpu.make_async_copy(others2, others2, f2_rsem).wait()
    total = jnp.zeros((1, LANES), F32)
    for s in range(NX * NC):
        total = total + fx[s]
    sizes[...] = jnp.sqrt(total * (1.0 / (L * 768 * NZ * NY * NC)))

    result.wait()
    pltpu.make_async_copy(others, others, f_ssem).wait()
    pltpu.make_async_copy(others2, others2, f2_ssem).wait()
    for it in range(ITERS):
        @pl.when(owner)
        def _():
            sent = part.at[it, pl.ds(0, GROUPS - 1)]
            pltpu.make_async_copy(sent, sent, rs_ssem.at[it]).wait()
            sent = xbuf.at[it, pl.ds(0, NX * NC - 1)]
            pltpu.make_async_copy(sent, sent, x_ssem.at[it]).wait()
            sent = edge.at[it, pl.ds(0, GROUPS - 1)]
            pltpu.make_async_copy(sent, sent, e_ssem.at[it]).wait()
            sent = rsbuf.at[0, pl.ds(0, NZ * NY - 1)]
            pltpu.make_async_copy(sent, sent, ag_ssem.at[it]).wait()

        @pl.when(jnp.logical_not(owner))
        def _():
            sent = part.at[it]
            pltpu.make_async_copy(sent, sent, rs_ssem.at[it]).wait()
            sent = edge.at[it]
            pltpu.make_async_copy(sent, sent, e_ssem.at[it]).wait()


def finish(u, row, relaxed, sizes, sem):
    copy = pltpu.make_async_copy(u, relaxed, sem)
    copy.start()
    sizes[...] = row[:, 0:ITERS]
    copy.wait()


def local(displacement, surface_load, dens_grad, dens_ref, relax_rate, basis, neighbours, green):
    vmem = pltpu.VMEM
    dma = pltpu.SemaphoreType.DMA
    scratch = [
        vmem((2432, 768), BF16),
        vmem(((DEG + 1) * L, L), F32),
        vmem((16, 768), F32),
        vmem((16, 768), F32),
        vmem((16, 768), F32),
        vmem((16, 768), F32),
        vmem((4, 768), jnp.int32),
        vmem((1, 16), F32),
        vmem((768, 768), BF16),
        vmem((16, 64, LANES), F32),
        vmem((LANES, LANES), BF16),
        vmem((16, 768), F32),
        vmem((ITERS, GROUPS, 16, LANES), BF16),
        vmem((ITERS, GROUPS, 2, LANES), F32),
        vmem((ITERS, NZ * NY, 16, LANES), BF16),
        vmem((ITERS, NZ * NY, 2, LANES), F32),
        vmem((ITERS, 24, LANES), F32),
        vmem((ITERS, NX * NC, 24, LANES), F32),
        vmem((ITERS, 16, LANES), BF16),
        vmem((ITERS, GROUPS, 16, LANES), BF16),
        vmem((1, 1, LANES), F32),
        vmem((NZ * NY, 1, LANES), F32),
        vmem((1, 1, LANES), F32),
        vmem((NX * NC, 1, LANES), F32),
        vmem((1, LANES), F32),
        dma((8,)), dma,
        dma((ITERS,)), dma((ITERS,)), dma((ITERS,)), dma((ITERS,)),
        dma((ITERS,)), dma((ITERS,)), dma((ITERS,)),
        dma((ITERS, GROUPS)),
        dma, dma, dma, dma,
    ]
    u, row = pl.pallas_call(
        kernel,
        out_shape=(
            jax.ShapeDtypeStruct((16, 768), F32),
            jax.ShapeDtypeStruct((1, LANES), F32),
        ),
        in_specs=[pl.BlockSpec(memory_space=pl.ANY)] * 8,
        out_specs=(
            pl.BlockSpec(memory_space=pl.ANY),
            pl.BlockSpec(memory_space=pltpu.VMEM),
        ),
        scratch_shapes=scratch,
        compiler_params=pltpu.CompilerParams(
            collective_id=0, has_side_effects=True, vmem_limit_bytes=56 << 20
        ),
        name="relaxation",
    )(
        displacement,
        surface_load,
        dens_grad,
        dens_ref.reshape(1, 16),
        relax_rate,
        basis,
        neighbours,
        green.reshape((DEG + 1) * L, L),
    )
    relaxed, sizes = pl.pallas_call(
        finish,
        out_shape=(
            jax.ShapeDtypeStruct((16, 768), F32),
            jax.ShapeDtypeStruct((1, ITERS), F32),
        ),
        in_specs=[
            pl.BlockSpec(memory_space=pl.ANY),
            pl.BlockSpec(memory_space=pltpu.VMEM),
        ],
        out_specs=(
            pl.BlockSpec(memory_space=pl.ANY),
            pl.BlockSpec(memory_space=pltpu.VMEM),
        ),
        scratch_shapes=[dma],
        name="finish",
    )(u, row)
    return relaxed, sizes.reshape(ITERS)


def solution(mesh):
    torus = Mesh(mesh.devices.reshape(NZ, NY, NC, NX), AXES)
    return jax.shard_map(
        local,
        mesh=torus,
        in_specs=(
            P("rad", LAT),
            P("rad", LAT),
            P("rad", LAT),
            P("rad"),
            P("rad", LAT),
            P(None, LAT),
            P(None, LAT),
            P(),
        ),
        out_specs=(P("rad", LAT), P()),
        check_vma=False,
    )
```

time: 108 us -> 99.1 us (0.918)
  Pallas kernels: 105 us -> 98.3 us
  local copies, waits for them, and re-layouts: 2.57 us -> 0 us
    pallas_call x1, Pallas kernels: 105 us -> 94.6 us  [local(): pl.pallas_call(kernel, out_shape=(jax.ShapeDtypeStruct((16, 768), F32), j...]
    pallas_call x0 -> x1, Pallas kernels: none -> 3.72 us  [local(): pl.pallas_call(finish, out_shape=(jax.ShapeDtypeStruct((16, 768), F32), j...]
    unnamed x1 -> x0, local copies, waits for them, and re-layouts: 1.42 us -> none
    squeeze x1 -> x0, local copies, waits for them, and re-layouts: 1.15 us -> none  [local(): return (relaxed, sizes[0, :ITERS])]
where the time goes in v1:
time: 99.1 us; the launch traced here: 99 us
  Pallas kernels  98.3 us (99%)
    pallas_call x1, Pallas kernels, local(): pl.pallas_call(kernel, out_shape=(jax.ShapeDtypeStruct((16, 768), F32), j...  94.6 us
    pallas_call x1, Pallas kernels, local(): pl.pallas_call(finish, out_shape=(jax.ShapeDtypeStruct((16, 768), F32), j...  3.72 us

profile of v1, /device:TPU:1, one launch (start us, length us, event | category | flops | bytes accessed | tf_op | source)
XLA Modules:
  0.0 99.0 jit_solution(12041646744883827844)
XLA Ops:
  0.6 94.6 %relaxation.1 = (f32[16,768]{1,0:T(8,128)}, f32[1,128]{1,0:T(1,128)}) custom-call(f32[16,768]{1,0:T(8,128)} %disp.1, f32[16,768]{1,0:T(8,128)} %load.1, f32[16,768]{1,0:T(8,128)} %grad.1, f32[1,16]{1,0:T(1,128)} %bitcast.4, f32[16,768]{1,0:T(8,128)} %rate.1, bf16[2432,768]{1,0:T(8,128)(2,1)} %basis_hbm.1, s32[4,768]{1,0:T(4,128)} %nbr.1, f32[3136,64]{1,0:T(8,128)} %bitcast.3), custom_call_target="tpu_custom_call" | custom-call | tf_op jit(solution)/shard_map/relaxation/pallas_call | solution.py:340
  95.2 3.7 %finish.1 = (f32[16,768]{1,0:T(8,128)}, f32[1,3]{1,0:T(1,128)}) custom-call(f32[16,768]{1,0:T(8,128)} %get-tuple-element.6.u, f32[1,128]{1,0:T(1,128)} %get-tuple-element.7.row), custom_call_target="tpu_custom_call" | custom-call | tf_op jit(solution)/shard_map/finish/pallas_call | solution.py:366

commit v2 on v1

--- a/solution.py
+++ b/solution.py
@@ -48,7 +48,7 @@
     disp, load, grad, dref, rate, basis_hbm, nbr, green_hbm,
     out, sizes,
     basis, green, u_s, ld_s, rt_s, gr_s, nbr_s, dref_s, count, gexp, onehot,
-    base, part, edge, rsbuf, edgebuf, xsend, xbuf, lsend, lbuf, fsend, fplane, fsend2, fx, sq_s,
+    base, part, edge, rsbuf, edgebuf, xsend, xbuf, lsend, lbuf, fsend, fplane, fsend2, fx, sq_s, delta_s,
     in_sem, out_sem, rs_ssem, rs_rsem, e_ssem, e_rsem, x_ssem, x_rsem, ag_ssem, ag_rsem,
     f_ssem, f_rsem, f2_ssem, f2_rsem,
 ):
@@ -117,8 +117,15 @@
         axis=0,
     )
     sq_s[...] = jnp.zeros((1, LANES), F32)
+    delta_s[...] = jnp.zeros((16, 768), F32)
 
     pl.semaphore_wait(barrier, len(plane_ids) + len(near_ids))
+
+    def add_squares(it):
+        square = delta_s[...] * delta_s[...]
+        square = jnp.sum(jnp.sum(square, axis=0, keepdims=True), axis=1, keepdims=True)
+        lane = lax.broadcasted_iota(jnp.int32, (1, LANES), 1)
+        sq_s[...] = jnp.where(lane == it, square, sq_s[...])
 
     def step(it, carry):
         u = u_s[...]
@@ -135,6 +142,7 @@
             )
             part[it, g] = tile[0:16].astype(BF16)
             edge[it, g] = tile[16:18]
+        for g in range(GROUPS):
             gz, gb = group_chip(g)
             dev = (gz, gb * 2 + c, c, x)
 
@@ -151,11 +159,6 @@
                     device_id=dev, device_id_type=MESH,
                 ).start()
 
-            @pl.when(g_own == g)
-            def _():
-                rsbuf[it, chip] = tile[0:16].astype(BF16)
-                edgebuf[it, chip] = tile[16:18]
-
         @pl.when(it == 0)
         def _():
             for copy in loads[4:]:
@@ -176,8 +179,12 @@
         lap = gathered[0:16] + gathered[16:32] - 4.0 * u
         base[...] = ld_s[...] + lap - u
 
+        add_squares(it - 1)
+
         @pl.when(owner)
         def _():
+            rsbuf[it, chip] = part[it, g_own]
+            edgebuf[it, chip] = edge[it, g_own]
             incoming = rsbuf.at[it, pl.ds(0, NZ * NY - 1)]
             pltpu.make_async_copy(incoming, incoming, rs_rsem.at[it]).wait()
             sums = [jnp.zeros((16, LANES), F32) for _ in range(4)]
@@ -225,26 +232,26 @@
             lbuf[it, g_own] = phi
 
         force = jnp.zeros((16, 768), F32)
-        for g in range(GROUPS):
-            @pl.when(g_own != g)
-            def _():
-                pltpu.make_async_copy(lbuf.at[it, g], lbuf.at[it, g], ag_rsem.at[it, g]).wait()
-
-            force = force + lax.dot_general(
-                lbuf[it, g], basis[g * LANES : (g + 1) * LANES, :], NN, preferred_element_type=F32
-            )
+        for groups in (range(0, 10), range(10, GROUPS)):
+            for g in groups:
+                @pl.when(g_own != g)
+                def _():
+                    pltpu.make_async_copy(lbuf.at[it, g], lbuf.at[it, g], ag_rsem.at[it, g]).wait()
+            for g in groups:
+                force = force + lax.dot_general(
+                    lbuf[it, g], basis[g * LANES : (g + 1) * LANES, :], NN,
+                    preferred_element_type=F32,
+                )
         delta = rt_s[...] * (base[...] + force)
-        u_s[...] = u_s[...] + delta
-        square = delta * delta
-        square = jnp.sum(jnp.sum(square, axis=0, keepdims=True), axis=1, keepdims=True)
-        lane = lax.broadcasted_iota(jnp.int32, (1, LANES), 1)
-        sq_s[...] = jnp.where(lane == it, square, sq_s[...])
+        delta_s[...] = delta
+        u_s[...] = u + delta
         return carry
 
     lax.fori_loop(0, ITERS, step, 0)
     result = pltpu.make_async_copy(u_s, out, out_sem)
     result.start()
 
+    add_squares(ITERS - 1)
     fsend[0] = sq_s[...]
     for dev in plane_ids:
         pltpu.make_async_remote_copy(
@@ -270,7 +277,7 @@
     total = jnp.zeros((1, LANES), F32)
     for s in range(NX * NC):
         total = total + fx[s]
-    sizes[...] = jnp.sqrt(total * (1.0 / (L * 768 * NZ * NY * NC)))
+    sizes[...] = jnp.sqrt(total * (1.0 / (L * 768 * NZ * NY * NC)))[:, 0:ITERS]
 
     result.wait()
     pltpu.make_async_copy(others, others, f_ssem).wait()
@@ -295,13 +302,6 @@
             pltpu.make_async_copy(sent, sent, e_ssem.at[it]).wait()
 
 
-def finish(u, row, relaxed, sizes, sem):
-    copy = pltpu.make_async_copy(u, relaxed, sem)
-    copy.start()
-    sizes[...] = row[:, 0:ITERS]
-    copy.wait()
-
-
 def local(displacement, surface_load, dens_grad, dens_ref, relax_rate, basis, neighbours, green):
     vmem = pltpu.VMEM
     dma = pltpu.SemaphoreType.DMA
@@ -331,17 +331,18 @@
         vmem((1, 1, LANES), F32),
         vmem((NX * NC, 1, LANES), F32),
         vmem((1, LANES), F32),
+        vmem((16, 768), F32),
         dma((8,)), dma,
         dma((ITERS,)), dma((ITERS,)), dma((ITERS,)), dma((ITERS,)),
         dma((ITERS,)), dma((ITERS,)), dma((ITERS,)),
         dma((ITERS, GROUPS)),
         dma, dma, dma, dma,
     ]
-    u, row = pl.pallas_call(
+    relaxed, sizes = pl.pallas_call(
         kernel,
         out_shape=(
             jax.ShapeDtypeStruct((16, 768), F32),
-            jax.ShapeDtypeStruct((1, LANES), F32),
+            jax.ShapeDtypeStruct((1, ITERS), F32),
         ),
         in_specs=[pl.BlockSpec(memory_space=pl.ANY)] * 8,
         out_specs=(
@@ -363,23 +364,6 @@
         neighbours,
         green.reshape((DEG + 1) * L, L),
     )
-    relaxed, sizes = pl.pallas_call(
-        finish,
-        out_shape=(
-            jax.ShapeDtypeStruct((16, 768), F32),
-            jax.ShapeDtypeStruct((1, ITERS), F32),
-        ),
-        in_specs=[
-            pl.BlockSpec(memory_space=pl.ANY),
-            pl.BlockSpec(memory_space=pltpu.VMEM),
-        ],
-        out_specs=(
-            pl.BlockSpec(memory_space=pl.ANY),
-            pl.BlockSpec(memory_space=pltpu.VMEM),
-        ),
-        scratch_shapes=[dma],
-        name="finish",
-    )(u, row)
     return relaxed, sizes.reshape(ITERS)
 
 

time: 99.1 us -> 93.7 us (0.946)
  Pallas kernels: 98.3 us -> 90.3 us
  local copies, waits for them, and re-layouts: 0 us -> 2.57 us
    pallas_call x1, Pallas kernels: 94.6 us -> 90.3 us  [local(): pl.pallas_call(kernel, out_shape=(jax.ShapeDtypeStruct((16, 768), F32), j...]
    pallas_call x1 -> x0, Pallas kernels: 3.72 us -> none  [local(): pl.pallas_call(finish, out_shape=(jax.ShapeDtypeStruct((16, 768), F32), j...]
    unnamed x0 -> x2, local copies, waits for them, and re-layouts: none -> 2.57 us
where the time goes in v2:
time: 93.7 us; the launch traced here: 93.6 us
  Pallas kernels  90.3 us (96%)
  local copies, waits for them, and re-layouts  2.57 us (3%)
    pallas_call x1, Pallas kernels, local(): pl.pallas_call(kernel, out_shape=(jax.ShapeDtypeStruct((16, 768), F32), j...  90.3 us
    unnamed x2, local copies, waits for them, and re-layouts  2.57 us

profile of v2, /device:TPU:1, one launch (start us, length us, event | category | flops | bytes accessed | tf_op | source)
XLA Modules:
  0.0 93.6 jit_solution(8302127656919829151)
XLA Ops:
  0.6 90.3 %relaxation.1 = (f32[16,768]{1,0:T(8,128)}, f32[1,3]{1,0:T(1,128)}) custom-call(f32[16,768]{1,0:T(8,128)} %disp.1, f32[16,768]{1,0:T(8,128)} %load.1, f32[16,768]{1,0:T(8,128)} %grad.1, f32[1,16]{1,0:T(1,128)} %bitcast.4, f32[16,768]{1,0:T(8,128)} %rate.1, bf16[2432,768]{1,0:T(8,128)(2,1)} %basis_hbm.1, s32[4,768]{1,0:T(4,128)} %nbr.1, f32[3136,64]{1,0:T(8,128)} %bitcast.3), custom_call_target="tpu_custom_call" | custom-call | tf_op jit(solution)/shard_map/relaxation/pallas_call | solution.py:341
  91.0 1.4 %copy.12 = f32[16,768]{1,0:T(8,128)} copy(f32[16,768]{1,0:T(8,128)} %get-tuple-element.8) | data formatting | bytes 98304
  92.4 1.1 %copy.13 = f32[3]{0:T(128)} copy(f32[3]{0:T(128)} %bitcast.5) | data formatting | bytes 24

commit v3 on v2

--- a/solution.py
+++ b/solution.py
@@ -15,7 +15,7 @@
 LANES = 128
 AXES = ("lz", "ly", "lc", "rad")
 LAT = AXES[:3]
-MESH = pl.DeviceIdType.MESH
+LOGICAL = pl.DeviceIdType.LOGICAL
 NT = (((1,), (1,)), ((), ()))
 NN = (((1,), (0,)), ((), ()))
 F32 = jnp.float32
@@ -27,45 +27,63 @@
 )
 
 
+def distance(o):
+    return min(o[0], NZ - o[0]) + min(o[1], NY - o[1])
+
+
+SERVED = [
+    o for o in [*PLANE, (0, 0)] if distance(o) < 4 or (distance(o) == 4 and o[0] < 4)
+]
+assert len(SERVED) == NZ * NY // 2
+
+
 def group_chip(g):
-    if g < 8:
-        return g, g % 4
-    if g < 16:
-        return g - 8, (g - 8 + 2) % 4
-    return (g - 16) * 3, ((g - 16) * 3 + 1) % 4
+    return g % 4, (3 * (g // 4) + 2 * (g % 4)) % NY
 
 
 def owned_group(z, y, core):
-    b = y // 2
-    g = jnp.where(b == z % 4, z, -1)
-    g = jnp.where(b == (z + 2) % 4, z + 8, g)
-    extra = (b == (z + 1) % 4) & (z % 3 == 0)
-    g = jnp.where(extra, z // 3 + 16, g)
-    return jnp.where(y % 2 == core, g, -1)
+    half_z, half_y = z & 3, (y - core + (z & 4)) & 7
+    owned = jnp.int32(-1)
+    for g in range(GROUPS):
+        gz, gy = group_chip(g)
+        owned = jnp.where((half_z == gz) & (half_y == gy), g, owned)
+    return owned
 
 
 def kernel(
     disp, load, grad, dref, rate, basis_hbm, nbr, green_hbm,
     out, sizes,
     basis, green, u_s, ld_s, rt_s, gr_s, nbr_s, dref_s, count, gexp, onehot,
-    base, part, edge, rsbuf, edgebuf, xsend, xbuf, lsend, lbuf, fsend, fplane, fsend2, fx, sq_s, delta_s,
-    in_sem, out_sem, rs_ssem, rs_rsem, e_ssem, e_rsem, x_ssem, x_rsem, ag_ssem, ag_rsem,
+    base, part, edge, rsbuf, edgebuf, xsend, xbuf, csend, cbuf, cedge, cedgebuf, lsend, lbuf, fsend, frow, fsend2, fz, sq_s, delta_s,
+    in_sem, out_sem, rs_ssem, rs_rsem, e_ssem, e_rsem, x_ssem, x_rsem, c_ssem, c_rsem, ce_ssem, ce_rsem, ag_ssem, ag_rsem,
     f_ssem, f_rsem, f2_ssem, f2_rsem,
 ):
     z, y, c, x = (lax.axis_index(a) for a in AXES)
     chip = z * NY + y
     g_own = owned_group(z, y, c)
     owner = g_own >= 0
-    other_y = 2 * (y // 2) + (1 - y % 2)
-
-    plane_ids = [((z + dz) % NZ, (y + dy) % NY, c, x) for dz, dy in PLANE]
-    same = [(z, y, c, (x + d) % NX) for d in (2, 1, 3)]
-    cross = [(z, other_y, 1 - c, (x + d) % NX) for d in (2, 1, 3, 0)]
-    near_ids = same + cross
-
+    other_y = (y + 1 - 2 * c) & 7
+    site_z = z & 4
+
+    own_lane = c * 4 + x
+    z_part = [((z + d) & 7) * 64 for d in range(NZ)]
+    y_part = [((y + d) & 7) * 8 + own_lane for d in range(NY)]
+    plane_ids = [z_part[dz] + y_part[dy] for dz, dy in PLANE]
+    served_ids = [z_part[dz] + y_part[dy] for dz, dy in SERVED[:-1]]
+    same = [z_part[0] + y_part[0] - x + ((x + d) & 3) for d in (2, 1, 3)]
+    cross = [z_part[0] + other_y * 8 + (1 - c) * 4 + ((x + d) & 3) for d in (2, 1, 3, 0)]
+    row_ids = [
+        z_part[0] + (y_part[dy] ^ bits) for dy in (4, 3, 5, 2, 6, 1, 7, 0)
+        for bits in (2, 6, 1, 3, 5, 7, 4, 0) if dy or bits
+    ]
+    column_ids = [z_part[dz] + y_part[0] for dz in (4, 3, 5, 2, 6, 1, 7)]
+
+    greeted_ids = [
+        z_part[0] + (y_part[dy] ^ bits) for dy in (4, 3, 5, 2, 6, 1, 7, 0) for bits in range(1, 8)
+    ]
     barrier = pltpu.get_barrier_semaphore()
-    for dev in plane_ids + near_ids:
-        pl.semaphore_signal(barrier, inc=1, device_id=dev, device_id_type=MESH)
+    for dev in plane_ids + greeted_ids:
+        pl.semaphore_signal(barrier, inc=1, device_id=dev, device_id_type=LOGICAL)
 
     loads = [
         pltpu.make_async_copy(disp, u_s, in_sem.at[0]),
@@ -119,7 +137,7 @@
     sq_s[...] = jnp.zeros((1, LANES), F32)
     delta_s[...] = jnp.zeros((16, 768), F32)
 
-    pl.semaphore_wait(barrier, len(plane_ids) + len(near_ids))
+    pl.semaphore_wait(barrier, len(plane_ids) + len(greeted_ids))
 
     def add_squares(it):
         square = delta_s[...] * delta_s[...]
@@ -136,28 +154,39 @@
         lines = jnp.concatenate([rho, u[0:1], u[15:16], jnp.zeros((14, 768), F32)], axis=0)
         lines = lines.astype(BF16)
 
-        for g in range(GROUPS):
+        def send_groups(groups):
+            for g in groups:
+                gz, gy = group_chip(g)
+                for at in range(2):
+                    dev = (gz + 4 * at) * 64 + ((gy + 4 * at) % NY * 8 + c * 8 & 63) + own_lane
+
+                    @pl.when((g_own != g) | (site_z != 4 * at))
+                    def _():
+                        pltpu.make_async_remote_copy(
+                            src_ref=part.at[it, g], dst_ref=rsbuf.at[it, chip],
+                            send_sem=rs_ssem.at[it], recv_sem=rs_rsem.at[it],
+                            device_id=dev, device_id_type=LOGICAL,
+                        ).start()
+                        pltpu.make_async_remote_copy(
+                            src_ref=edge.at[it, g], dst_ref=edgebuf.at[it, chip],
+                            send_sem=e_ssem.at[it], recv_sem=e_rsem.at[it],
+                            device_id=dev, device_id_type=LOGICAL,
+                        ).start()
+
+        for g in range(0, 10):
             tile = lax.dot_general(
                 lines, basis[g * LANES : (g + 1) * LANES, :], NT, preferred_element_type=F32
             )
             part[it, g] = tile[0:16].astype(BF16)
             edge[it, g] = tile[16:18]
-        for g in range(GROUPS):
-            gz, gb = group_chip(g)
-            dev = (gz, gb * 2 + c, c, x)
-
-            @pl.when(g_own != g)
-            def _():
-                pltpu.make_async_remote_copy(
-                    src_ref=part.at[it, g], dst_ref=rsbuf.at[it, chip],
-                    send_sem=rs_ssem.at[it], recv_sem=rs_rsem.at[it],
-                    device_id=dev, device_id_type=MESH,
-                ).start()
-                pltpu.make_async_remote_copy(
-                    src_ref=edge.at[it, g], dst_ref=edgebuf.at[it, chip],
-                    send_sem=e_ssem.at[it], recv_sem=e_rsem.at[it],
-                    device_id=dev, device_id_type=MESH,
-                ).start()
+        send_groups(range(0, 10))
+        for g in range(10, GROUPS):
+            tile = lax.dot_general(
+                lines, basis[g * LANES : (g + 1) * LANES, :], NT, preferred_element_type=F32
+            )
+            part[it, g] = tile[0:16].astype(BF16)
+            edge[it, g] = tile[16:18]
+        send_groups(range(10, GROUPS))
 
         @pl.when(it == 0)
         def _():
@@ -197,37 +226,52 @@
             for s in range(NZ * NY):
                 sums[s % 4] = sums[s % 4] + edgebuf[it, s]
             edge_total = (sums[0] + sums[1]) + (sums[2] + sums[3])
-            total = jnp.concatenate([total, edge_total, ends], axis=0)
-            xsend[it] = total
-            me = x * NC + c
-            for dev in near_ids:
+            own = jnp.concatenate([total, edge_total, ends], axis=0)
+            xsend[it] = own
+            csend[it] = total.astype(BF16)
+            cedge[it] = edge_total
+            for dev in same:
                 pltpu.make_async_remote_copy(
-                    src_ref=xsend.at[it], dst_ref=xbuf.at[it, me],
+                    src_ref=xsend.at[it], dst_ref=xbuf.at[it, x],
                     send_sem=x_ssem.at[it], recv_sem=x_rsem.at[it],
-                    device_id=dev, device_id_type=MESH,
+                    device_id=dev, device_id_type=LOGICAL,
                 ).start()
-            xbuf[it, me] = total
-            others = xbuf.at[it, pl.ds(0, NX * NC - 1)]
+            for dev in cross:
+                pltpu.make_async_remote_copy(
+                    src_ref=csend.at[it], dst_ref=cbuf.at[it, x],
+                    send_sem=c_ssem.at[it], recv_sem=c_rsem.at[it],
+                    device_id=dev, device_id_type=LOGICAL,
+                ).start()
+                pltpu.make_async_remote_copy(
+                    src_ref=cedge.at[it], dst_ref=cedgebuf.at[it, x],
+                    send_sem=ce_ssem.at[it], recv_sem=ce_rsem.at[it],
+                    device_id=dev, device_id_type=LOGICAL,
+                ).start()
+            xbuf[it, x] = own
+            others = xbuf.at[it, pl.ds(0, NX - 1)]
             pltpu.make_async_copy(others, others, x_rsem.at[it]).wait()
-            blocks = [xbuf[it, 2 * b] + xbuf[it, 2 * b + 1] for b in range(NX)]
+            pltpu.make_async_copy(cbuf.at[it], cbuf.at[it], c_rsem.at[it]).wait()
+            pltpu.make_async_copy(cedgebuf.at[it], cedgebuf.at[it], ce_rsem.at[it]).wait()
+            blocks = [xbuf[it, b, 0:16] + cbuf[it, b].astype(F32) for b in range(NX)]
+            outer = [xbuf[it, b, 16:18] + cedgebuf[it, b] for b in range(NX)]
             rows = []
             for b in range(NX):
                 first, last = jnp.zeros((1, LANES), F32), jnp.zeros((1, LANES), F32)
                 if b > 0:
-                    first = -0.5 * blocks[b][18:19] * blocks[b - 1][17:18]
+                    first = -xbuf[it, b, 18:19] * outer[b - 1][1:2]
                 if b < NX - 1:
-                    last = 0.5 * blocks[b][19:20] * blocks[b + 1][16:17]
+                    last = xbuf[it, b, 19:20] * outer[b + 1][0:1]
                 mid = jnp.zeros((14, LANES), F32)
-                rows.append(blocks[b][0:16] + jnp.concatenate([first, mid, last], axis=0))
+                rows.append(blocks[b] + jnp.concatenate([first, mid, last], axis=0))
             coefs = jnp.concatenate(rows, axis=0)
             rows = [jnp.sum(gexp[i] * coefs, axis=0, keepdims=True) for i in range(16)]
             phi = jnp.concatenate(rows, axis=0).astype(BF16)
             lsend[it] = phi
-            for dev in plane_ids:
+            for dev in served_ids:
                 pltpu.make_async_remote_copy(
                     src_ref=lsend.at[it], dst_ref=lbuf.at[it, g_own],
                     send_sem=ag_ssem.at[it], recv_sem=ag_rsem.at[it, g_own],
-                    device_id=dev, device_id_type=MESH,
+                    device_id=dev, device_id_type=LOGICAL,
                 ).start()
             lbuf[it, g_own] = phi
 
@@ -253,30 +297,30 @@
 
     add_squares(ITERS - 1)
     fsend[0] = sq_s[...]
-    for dev in plane_ids:
+    me = y * 8 + c * 4 + x
+    for dev in row_ids:
         pltpu.make_async_remote_copy(
-            src_ref=fsend.at[0], dst_ref=fplane.at[chip], send_sem=f_ssem, recv_sem=f_rsem,
-            device_id=dev, device_id_type=MESH,
+            src_ref=fsend.at[0], dst_ref=frow.at[me], send_sem=f_ssem, recv_sem=f_rsem,
+            device_id=dev, device_id_type=LOGICAL,
         ).start()
-    fplane[chip] = sq_s[...]
-    others = fplane.at[pl.ds(0, NZ * NY - 1)]
+    frow[me] = sq_s[...]
+    others = frow.at[pl.ds(0, NY * NC * NX - 1)]
     pltpu.make_async_copy(others, others, f_rsem).wait()
     total = jnp.zeros((1, LANES), F32)
-    for s in range(NZ * NY):
-        total = total + fplane[s]
+    for s in range(NY * NC * NX):
+        total = total + frow[s]
     fsend2[0] = total
-    me = x * NC + c
-    for dev in near_ids:
+    for dev in column_ids:
         pltpu.make_async_remote_copy(
-            src_ref=fsend2.at[0], dst_ref=fx.at[me], send_sem=f2_ssem, recv_sem=f2_rsem,
-            device_id=dev, device_id_type=MESH,
+            src_ref=fsend2.at[0], dst_ref=fz.at[z], send_sem=f2_ssem, recv_sem=f2_rsem,
+            device_id=dev, device_id_type=LOGICAL,
         ).start()
-    fx[me] = total
-    others2 = fx.at[pl.ds(0, NX * NC - 1)]
+    fz[z] = total
+    others2 = fz.at[pl.ds(0, NZ - 1)]
     pltpu.make_async_copy(others2, others2, f2_rsem).wait()
     total = jnp.zeros((1, LANES), F32)
-    for s in range(NX * NC):
-        total = total + fx[s]
+    for s in range(NZ):
+        total = total + fz[s]
     sizes[...] = jnp.sqrt(total * (1.0 / (L * 768 * NZ * NY * NC)))[:, 0:ITERS]
 
     result.wait()
@@ -285,20 +329,22 @@
     for it in range(ITERS):
         @pl.when(owner)
         def _():
-            sent = part.at[it, pl.ds(0, GROUPS - 1)]
+            sent = rsbuf.at[0, pl.ds(0, 2 * GROUPS - 1)]
             pltpu.make_async_copy(sent, sent, rs_ssem.at[it]).wait()
-            sent = xbuf.at[it, pl.ds(0, NX * NC - 1)]
+            sent = xbuf.at[it, pl.ds(0, NX - 1)]
             pltpu.make_async_copy(sent, sent, x_ssem.at[it]).wait()
-            sent = edge.at[it, pl.ds(0, GROUPS - 1)]
+            pltpu.make_async_copy(cbuf.at[it], cbuf.at[it], c_ssem.at[it]).wait()
+            pltpu.make_async_copy(cedgebuf.at[it], cedgebuf.at[it], ce_ssem.at[it]).wait()
+            sent = edgebuf.at[0, pl.ds(0, 2 * GROUPS - 1)]
             pltpu.make_async_copy(sent, sent, e_ssem.at[it]).wait()
-            sent = rsbuf.at[0, pl.ds(0, NZ * NY - 1)]
+            sent = rsbuf.at[0, pl.ds(0, NZ * NY // 2 - 1)]
             pltpu.make_async_copy(sent, sent, ag_ssem.at[it]).wait()
 
         @pl.when(jnp.logical_not(owner))
         def _():
-            sent = part.at[it]
+            sent = rsbuf.at[0, pl.ds(0, 2 * GROUPS)]
             pltpu.make_async_copy(sent, sent, rs_ssem.at[it]).wait()
-            sent = edge.at[it]
+            sent = edgebuf.at[0, pl.ds(0, 2 * GROUPS)]
             pltpu.make_async_copy(sent, sent, e_ssem.at[it]).wait()
 
 
@@ -323,16 +369,21 @@
         vmem((ITERS, NZ * NY, 16, LANES), BF16),
         vmem((ITERS, NZ * NY, 2, LANES), F32),
         vmem((ITERS, 24, LANES), F32),
-        vmem((ITERS, NX * NC, 24, LANES), F32),
+        vmem((ITERS, NX, 24, LANES), F32),
+        vmem((ITERS, 16, LANES), BF16),
+        vmem((ITERS, NX, 16, LANES), BF16),
+        vmem((ITERS, 2, LANES), F32),
+        vmem((ITERS, NX, 2, LANES), F32),
         vmem((ITERS, 16, LANES), BF16),
         vmem((ITERS, GROUPS, 16, LANES), BF16),
         vmem((1, 1, LANES), F32),
         vmem((NZ * NY, 1, LANES), F32),
         vmem((1, 1, LANES), F32),
-        vmem((NX * NC, 1, LANES), F32),
+        vmem((NZ, 1, LANES), F32),
         vmem((1, LANES), F32),
         vmem((16, 768), F32),
         dma((8,)), dma,
+        dma((ITERS,)), dma((ITERS,)), dma((ITERS,)), dma((ITERS,)),
         dma((ITERS,)), dma((ITERS,)), dma((ITERS,)), dma((ITERS,)),
         dma((ITERS,)), dma((ITERS,)), dma((ITERS,)),
         dma((ITERS, GROUPS)),

time: 93.7 us -> 90.6 us (0.967)
  Pallas kernels: 90.3 us -> 87.2 us
    pallas_call x1, Pallas kernels: 90.3 us -> 87.2 us  [local(): pl.pallas_call(kernel, out_shape=(jax.ShapeDtypeStruct((16, 768), F32), j...]
where the time goes in v3:
time: 90.6 us; the launch traced here: 90.4 us
  Pallas kernels  87.2 us (96%)
  local copies, waits for them, and re-layouts  2.57 us (3%)
    pallas_call x1, Pallas kernels, local(): pl.pallas_call(kernel, out_shape=(jax.ShapeDtypeStruct((16, 768), F32), j...  87.2 us
    unnamed x2, local copies, waits for them, and re-layouts  2.57 us

profile of v3, /device:TPU:1, one launch (start us, length us, event | category | flops | bytes accessed | tf_op | source)
XLA Modules:
  0.0 90.4 jit_solution(14724022276077020195)
XLA Ops:
  0.6 87.2 %relaxation.1 = (f32[16,768]{1,0:T(8,128)}, f32[1,3]{1,0:T(1,128)}) custom-call(f32[16,768]{1,0:T(8,128)} %disp.1, f32[16,768]{1,0:T(8,128)} %load.1, f32[16,768]{1,0:T(8,128)} %grad.1, f32[1,16]{1,0:T(1,128)} %bitcast.4, f32[16,768]{1,0:T(8,128)} %rate.1, bf16[2432,768]{1,0:T(8,128)(2,1)} %basis_hbm.1, s32[4,768]{1,0:T(4,128)} %nbr.1, f32[3136,64]{1,0:T(8,128)} %bitcast.3), custom_call_target="tpu_custom_call" | custom-call | tf_op jit(solution)/shard_map/relaxation/pallas_call | solution.py:392
  87.9 1.4 %copy.12 = f32[16,768]{1,0:T(8,128)} copy(f32[16,768]{1,0:T(8,128)} %get-tuple-element.8) | data formatting | bytes 98304
  89.3 1.1 %copy.13 = f32[3]{0:T(128)} copy(f32[3]{0:T(128)} %bitcast.5) | data formatting | bytes 24

commit v4 on v3

--- a/solution.py
+++ b/solution.py
@@ -193,14 +193,6 @@
             for copy in loads[4:]:
                 copy.wait()
             lax.fori_loop(0, 12, count_rows, 0)
-
-            @pl.when(owner)
-            def _():
-                k = g_own * LANES + lax.broadcasted_iota(jnp.int32, (LANES, LANES), 1)
-                d = lax.broadcasted_iota(jnp.int32, (LANES, LANES), 0) % 64
-                hit = (k >= d * d) & (k < (d + 1) * (d + 1)) & (k < KH)
-                onehot[...] = jnp.where(hit, 1.0, 0.0).astype(BF16)
-                lax.fori_loop(0, 16, expand, 0)
 
         high = u.astype(BF16).astype(F32)
         halves = jnp.concatenate([high, u - high], axis=0).astype(BF16)
@@ -248,6 +240,15 @@
                     device_id=dev, device_id_type=LOGICAL,
                 ).start()
             xbuf[it, x] = own
+
+            @pl.when(it == 0)
+            def _():
+                k = g_own * LANES + lax.broadcasted_iota(jnp.int32, (LANES, LANES), 1)
+                d = lax.broadcasted_iota(jnp.int32, (LANES, LANES), 0) % 64
+                hit = (k >= d * d) & (k < (d + 1) * (d + 1)) & (k < KH)
+                onehot[...] = jnp.where(hit, 1.0, 0.0).astype(BF16)
+                lax.fori_loop(0, 16, expand, 0, unroll=4)
+
             others = xbuf.at[it, pl.ds(0, NX - 1)]
             pltpu.make_async_copy(others, others, x_rsem.at[it]).wait()
             pltpu.make_async_copy(cbuf.at[it], cbuf.at[it], c_rsem.at[it]).wait()

time: 90.6 us -> 90.1 us (level)
  no operation moved by 1% of the time
where the time goes in v4:
time: 90.1 us; the launch traced here: 89.9 us
  Pallas kernels  86.7 us (96%)
  local copies, waits for them, and re-layouts  2.57 us (3%)
    pallas_call x1, Pallas kernels, local(): pl.pallas_call(kernel, out_shape=(jax.ShapeDtypeStruct((16, 768), F32), j...  86.7 us
    unnamed x2, local copies, waits for them, and re-layouts  2.57 us

profile of v4, /device:TPU:1, one launch (start us, length us, event | category | flops | bytes accessed | tf_op | source)
XLA Modules:
  0.0 89.9 jit_solution(4628721077056243899)
XLA Ops:
  0.6 86.7 %relaxation.1 = (f32[16,768]{1,0:T(8,128)}, f32[1,3]{1,0:T(1,128)}) custom-call(f32[16,768]{1,0:T(8,128)} %disp.1, f32[16,768]{1,0:T(8,128)} %load.1, f32[16,768]{1,0:T(8,128)} %grad.1, f32[1,16]{1,0:T(1,128)} %bitcast.4, f32[16,768]{1,0:T(8,128)} %rate.1, bf16[2432,768]{1,0:T(8,128)(2,1)} %basis_hbm.1, s32[4,768]{1,0:T(4,128)} %nbr.1, f32[3136,64]{1,0:T(8,128)} %bitcast.3), custom_call_target="tpu_custom_call" | custom-call | tf_op jit(solution)/shard_map/relaxation/pallas_call | solution.py:393
  87.3 1.4 %copy.12 = f32[16,768]{1,0:T(8,128)} copy(f32[16,768]{1,0:T(8,128)} %get-tuple-element.8) | data formatting | bytes 98304
  88.8 1.1 %copy.13 = f32[3]{0:T(128)} copy(f32[3]{0:T(128)} %bitcast.5) | data formatting | bytes 24
